TPU v7x, 512 devices: a whole 4x4x16 slice. The times are simulated.
512 devices in a mesh: dp: 4 (over z_hi), fsdp: 8 (over x, core), tensor: 16 (over z_lo, y).
Axes of the slice: x: 4, y: 4, z: 16 (z_hi: 4, z_lo: 4; z = z_hi * 4 + z_lo), core: 2. Of those that a mesh axis runs over, the one named last changes fastest.
Arguments:
- features: bfloat16 [8192, 8192], P(('dp', 'fsdp'), 'tensor'), may hold values from -6 to 6
- cotangent: bfloat16 [8192, 32768], P(('dp', 'fsdp'), 'tensor'), may hold values from -6 to 6
- butterfly: bfloat16 [8, 128, 64, 256], P(None, 'tensor', 'fsdp'), may hold values from -0.25 to 0.25
- left_factor: bfloat16 [8192, 256], P('tensor', 'fsdp'), may hold values from -0.0625 to 0.0625
- right_factor: bfloat16 [256, 32768], P('fsdp', 'tensor'), may hold values from -0.375 to 0.375
Outputs:
- activation: bfloat16 [8192, 32768], P(('dp', 'fsdp'), 'tensor')
- feature_grad: bfloat16 [8192, 8192], P(('dp', 'fsdp'), 'tensor')
- butterfly_grad: float32 [8, 128, 64, 256], P(None, 'tensor', 'fsdp')
- left_grad: float32 [8192, 256], P('tensor', 'fsdp')
- right_grad: float32 [256, 32768], P('fsdp', 'tensor')
All inputs are finite; a program needn't handle non-finite values.
Results may differ from a plain program's by a relative error of at most 0.017.
Values may be sent and summed in bfloat16 or wider, within the bound.
A program may use at most 64 MiB of HBM per device.

v0:
```python
import jax
import jax.numpy as jnp
from jax import lax
from jax.sharding import PartitionSpec as P


def swapped(shard, axis, distance):
    return lax.ppermute(shard, axis, [(i, i ^ 1 << distance) for i in range(lax.axis_size(axis))])


def flip_groups(array, level):
    stride = 1 << level
    shape = array.shape
    split = array.reshape((shape[0], shape[1] // (2 * stride), 2, stride) + shape[2:])
    return jnp.flip(split, axis=2).reshape(shape)


def local(features, cotangent, butterfly, left_factor, right_factor):
    tok_rows, local_width = features.shape
    local_groups = butterfly.shape[1]
    block_width = local_width // local_groups
    hidden_block = butterfly.shape[3]
    local_bits = local_groups.bit_length() - 1
    tensor_bits = lax.axis_size("tensor").bit_length() - 1
    all_bits = local_bits + tensor_bits
    weight_all, left_all, right_all = (
        lax.all_gather(butterfly, "fsdp", axis=2, tiled=True),
        lax.all_gather(left_factor, "fsdp", axis=1, tiled=True),
        lax.all_gather(right_factor, "fsdp", axis=0, tiled=True),
    )
    grouped = features.reshape(tok_rows, local_groups, block_width)
    partners = [grouped]
    for level in range(all_bits):
        if level < local_bits:
            partners.append(flip_groups(grouped, level))
        else:
            remote = swapped(features, "tensor", level - local_bits)
            partners.append(remote.reshape(tok_rows, local_groups, block_width))
    pre = jnp.zeros((tok_rows, local_groups, hidden_block), jnp.float32)
    for term_idx in range(all_bits + 1):
        pre = pre + jnp.einsum(
            "ngb,gbh->ngh",
            partners[term_idx],
            weight_all[term_idx],
            preferred_element_type=jnp.float32,
        )
    low_part = jnp.dot(features, left_all, preferred_element_type=jnp.float32)
    lowrank = lax.psum(low_part, "tensor").astype(jnp.bfloat16)
    pre = pre.reshape(tok_rows, local_groups * hidden_block) + jnp.dot(
        lowrank, right_all, preferred_element_type=jnp.float32
    )
    act, pull = jax.vjp(jax.nn.gelu, pre)
    activation = act.astype(jnp.bfloat16)
    gpre = pull(cotangent.astype(jnp.float32))[0].astype(jnp.bfloat16)
    gpre_grouped = gpre.reshape(tok_rows, local_groups, hidden_block)
    part_bfly = jnp.stack(
        [
            jnp.einsum(
                "ngb,ngh->gbh", partners[term_idx], gpre_grouped, preferred_element_type=jnp.float32
            )
            for term_idx in range(all_bits + 1)
        ]
    ).astype(jnp.bfloat16)
    glow_part = jnp.dot(gpre, right_all.T, preferred_element_type=jnp.float32)
    glow = lax.psum(glow_part, "tensor").astype(jnp.bfloat16)
    part_left = jnp.dot(features.T, glow, preferred_element_type=jnp.float32).astype(jnp.bfloat16)
    part_right = jnp.dot(lowrank.T, gpre, preferred_element_type=jnp.float32).astype(jnp.bfloat16)
    dfeat = jnp.dot(glow, left_all.T, preferred_element_type=jnp.float32)
    for term_idx in range(all_bits + 1):
        term = jnp.einsum(
            "ngh,gbh->ngb", gpre_grouped, weight_all[term_idx], preferred_element_type=jnp.float32
        )
        if term_idx > 0:
            level = term_idx - 1
            if level < local_bits:
                term = flip_groups(term, level)
            else:
                term = swapped(term.astype(jnp.bfloat16), "tensor", level - local_bits).astype(
                    jnp.float32
                )
        dfeat = dfeat + term.reshape(tok_rows, local_width)
    feature_grad = dfeat.astype(jnp.bfloat16)
    shard_bfly, shard_left, shard_right = (
        lax.psum_scatter(part_bfly, "fsdp", scatter_dimension=2, tiled=True).astype(jnp.float32),
        lax.psum_scatter(part_left, "fsdp", scatter_dimension=1, tiled=True).astype(jnp.float32),
        lax.psum_scatter(part_right, "fsdp", scatter_dimension=0, tiled=True).astype(jnp.float32),
    )
    grad_bfly, grad_left, grad_right = lax.psum((shard_bfly, shard_left, shard_right), "dp")
    return (activation, feature_grad, grad_bfly, grad_left, grad_right)


def solution(mesh):
    in_specs = (
        P(("dp", "fsdp"), "tensor"),
        P(("dp", "fsdp"), "tensor"),
        P(None, "tensor", "fsdp", None),
        P("tensor", "fsdp"),
        P("fsdp", "tensor"),
    )
    out_specs = (
        P(("dp", "fsdp"), "tensor"),
        P(("dp", "fsdp"), "tensor"),
        P(None, "tensor", "fsdp", None),
        P("tensor", "fsdp"),
        P("fsdp", "tensor"),
    )
    return jax.shard_map(local, mesh=mesh, in_specs=in_specs, out_specs=out_specs, check_vma=False)
```

profile of v0, /device:TPU:1, one launch (start us, length us, event | category | flops | bytes accessed | tf_op | source)
XLA Modules:
  0.0 400.7 jit_solution(11067036065175690493)
XLA Ops:
  8.0 4.0 %collective-permute-start = (bf16[256,512]{1,0:T(8,128)(2,1)}, bf16[256,512]{1,0:T(8,128)(2,1)S(1)}, u32[]{:S(2)}, u32[]{:S(2)}) collective-permute-start(bf16[256,512]{1,0:T(8,128)(2,1)} %param.5), channel_id=1, source_target_pairs={{0,1},{1,0},{2,3},{3,2},{4,5},{5,4},{6,7},{7,6},{8,9},{9,8},{10,11... | collective-permute-start | bytes 786440 | tf_op jit(solution)/shard_map/ppermute | solution.py:8
  12.0 4.5 %collective-permute-start.1 = (bf16[256,512]{1,0:T(8,128)(2,1)}, bf16[256,512]{1,0:T(8,128)(2,1)S(1)}, u32[]{:S(2)}, u32[]{:S(2)}) collective-permute-start(bf16[256,512]{1,0:T(8,128)(2,1)} %param.5), channel_id=1, source_target_pairs={{0,2},{1,3},{2,0},{3,1},{4,6},{5,7},{6,4},{7,5},{8,10},{9,11},{10,... | collective-permute-start | bytes 786440 | tf_op jit(solution)/shard_map/ppermute | solution.py:8
  16.5 3.5 collective-permute-start.2
  20.1 4.9 %collective-permute-start.3 = (bf16[256,512]{1,0:T(8,128)(2,1)}, bf16[256,512]{1,0:T(8,128)(2,1)S(1)}, u32[]{:S(2)}, u32[]{:S(2)}) collective-permute-start(bf16[256,512]{1,0:T(8,128)(2,1)} %param.5), channel_id=1, source_target_pairs={{0,8},{1,9},{2,10},{3,11},{4,12},{5,13},{6,14},{7,15},{8,0},{9,1},... | collective-permute-start | bytes 786440 | tf_op jit(solution)/shard_map/ppermute | solution.py:8
  26.3 14.9 %all_gather.10 = bf16[512,256]{0,1:T(8,128)(2,1)S(1)} all-gather(bf16[512,32]{0,1:T(8,128)(2,1)S(1)} %copy-done.16), channel_id=1, replica_groups=mesh['dp'=4,'fsdp'=8,'tensor'=16] {'fsdp'}, dimensions={1}, use_global_device_ids=true | all-gather | bytes 294912 | tf_op jit(solution)/shard_map/all_gather | solution.py:28
  41.4 66.5 %all-reduce.7 = bf16[256,256]{1,0:T(8,128)(2,1)S(1)} all-reduce(f32[256,256]{1,0:T(8,128)S(1)} %fusion.82), channel_id=1, replica_groups=mesh['dp'=4,'fsdp'=8,'tensor'=16] {'tensor'}, use_global_device_ids=true, to_apply=%region_0.1 | all-reduce | flops 65536 | bytes 393216 | tf_op jit(solution)/shard_map/psum | solution.py:48
  114.1 1.8 copy.85
  116.0 5.1 %fusion.2 = (bf16[256,2048]{1,0:T(8,128)(2,1)S(1)}, bf16[256,2048]{1,0:T(8,128)(2,1)}) fusion(bf16[256,2048]{1,0:T(8,128)(2,1)} %param.6, f32[256,2048]{1,0:T(8,128)} %copy.85, bf16[256,256]{1,0:T(8,128)(2,1)S(1)} %all-reduce.7, bf16[256,2048]{1,0:T(8,128)(2,1)} %all-gather.5.cloned.1.call-done), kind=kOutput, calls=%fused_computation.8 | convolution fusion | flops 281018368 | bytes 6422528 | tf_op jit(solution)/shard_map/dot_general | solution.py:49
  127.1 62.8 %all-reduce.8 = bf16[256,256]{1,0:T(8,128)(2,1)S(1)} all-reduce(f32[256,256]{1,0:T(8,128)S(1)} %fusion.83), channel_id=1, replica_groups=mesh['dp'=4,'fsdp'=8,'tensor'=16] {'tensor'}, use_global_device_ids=true, to_apply=%region_1.2 | all-reduce | flops 65536 | bytes 393216 | tf_op jit(solution)/shard_map/psum | solution.py:65
  195.4 2.2 fusion.46
  197.6 2.2 fusion.52
  199.8 2.1 fusion.14
  204.5 2.0 copy.87
  206.6 1.9 collective-permute-start.4
  209.9 2.1 collective-permute-start.5
  213.3 1.9 collective-permute-start.6
  215.3 2.1 fusion.17
  217.4 5.9 %collective-permute-start.7 = (bf16[256,8,64]{0,2,1:T(8,128)(2,1)}, bf16[256,8,64]{0,2,1:T(8,128)(2,1)S(1)}, u32[]{:S(2)}, u32[]{:S(2)}) collective-permute-start(bf16[256,8,64]{0,2,1:T(8,128)(2,1)} %fusion.17), channel_id=1, source_target_pairs={{0,8},{1,9},{2,10},{3,11},{4,12},{5,13},{6,14},{7,15},{8,0},{9,1},... | collective-permute-start | bytes 786440 | tf_op jit(solution)/shard_map/ppermute | solution.py:8
  227.3 2.5 collective-permute-done.7
  231.0 20.4 %reduce-scatter.6.cloned.1.call-done = bf16[512,32]{0,1:T(8,128)(2,1)} async-done(((bf16[512,256]{0,1:T(8,128)(2,1)}), bf16[512,32]{0,1:T(8,128)(2,1)}) %reduce-scatter.6.cloned.1.call-update) | async-done | bytes 32784 | tf_op jit(solution)/shard_map/reduce_scatter | solution.py:85
  251.5 41.2 %reduce-scatter.8.cloned.1.call-done = bf16[32,2048]{1,0:T(8,128)(2,1)} async-done(((bf16[256,2048]{1,0:T(8,128)(2,1)}), bf16[32,2048]{1,0:T(8,128)(2,1)}) %reduce-scatter.8.cloned.1.call-update) | async-done | bytes 131088 | tf_op jit(solution)/shard_map/reduce_scatter | solution.py:86
  292.7 42.8 %all-reduce.9 = (f32[512,32]{0,1:T(8,128)}, f32[32,2048]{1,0:T(8,128)}) all-reduce(bf16[512,32]{0,1:T(8,128)(2,1)} %reduce-scatter.6.cloned.1.call-done, bf16[32,2048]{1,0:T(8,128)(2,1)} %reduce-scatter.8.cloned.1.call-done), channel_id=1, replica_groups=mesh['dp'=4,'fsdp'=8,'tensor'=16] {'dp'}, use_global_device_ids=true, to_apply=%region_5.6 | all-reduce | flops 81920 | bytes 491520 | tf_op jit(solution)/shard_map/psum | solution.py:88
  335.5 56.5 %all-reduce.6.cloned.1.call-done = f32[8,8,8,256]{3,2,1,0:T(8,128)} async-done(((f32[8,8,8,256]{3,2,1,0:T(8,128)}), f32[8,8,8,256]{3,2,1,0:T(8,128)}) %all-reduce.6.cloned.1.call-update) | async-done | bytes 524304 | tf_op jit(solution)/shard_map/psum | solution.py:88
  392.0 1.9 copy.199
  (107 shorter events, 29.9 us)
Async XLA Ops:
  7.2 34.0 %copy-start = (bf16[256,512]{1,0:T(8,128)(2,1)S(1)}, bf16[256,512]{1,0:T(8,128)(2,1)}, u32[]{:S(2)}) copy-start(bf16[256,512]{1,0:T(8,128)(2,1)} %param.5) | copy-start | bytes 786436
  7.2 19.1 %copy-start.16 = (bf16[512,32]{0,1:T(8,128)(2,1)S(1)}, bf16[512,32]{0,1:T(8,128)(2,1)}, u32[]{:S(2)}) copy-start(bf16[512,32]{0,1:T(8,128)(2,1)} %param.8) | copy-start | bytes 98308
  7.2 101.5 %all-gather.3.cloned.1.call-start = ((), (), s32[]{:S(2)}) async-start(), calls=%async_computation.3 | async-start | bytes 2359296 | tf_op jit(solution)/shard_map/all_gather | solution.py:27
  7.9 108.0 %all-gather.5.cloned.1.call-start = ((), (), s32[]{:S(2)}) async-start(), calls=%async_computation.4 | async-start | bytes 1179648 | tf_op jit(solution)/shard_map/all_gather | solution.py:29
  8.0 100.0 %collective-permute-start = (bf16[256,512]{1,0:T(8,128)(2,1)}, bf16[256,512]{1,0:T(8,128)(2,1)S(1)}, u32[]{:S(2)}, u32[]{:S(2)}) collective-permute-start(bf16[256,512]{1,0:T(8,128)(2,1)} %param.5), channel_id=1, source_target_pairs={{0,1},{1,0},{2,3},{3,2},{4,5},{5,4},{6,7},{7,6},{8,9},{9,8},{10,11... | collective-permute-start | bytes 786440 | tf_op jit(solution)/shard_map/ppermute | solution.py:8
  12.0 96.2 %collective-permute-start.1 = (bf16[256,512]{1,0:T(8,128)(2,1)}, bf16[256,512]{1,0:T(8,128)(2,1)S(1)}, u32[]{:S(2)}, u32[]{:S(2)}) collective-permute-start(bf16[256,512]{1,0:T(8,128)(2,1)} %param.5), channel_id=1, source_target_pairs={{0,2},{1,3},{2,0},{3,1},{4,6},{5,7},{6,4},{7,5},{8,10},{9,11},{10,... | collective-permute-start | bytes 786440 | tf_op jit(solution)/shard_map/ppermute | solution.py:8
  16.5 91.8 %collective-permute-start.2 = (bf16[256,512]{1,0:T(8,128)(2,1)}, bf16[256,512]{1,0:T(8,128)(2,1)S(1)}, u32[]{:S(2)}, u32[]{:S(2)}) collective-permute-start(bf16[256,512]{1,0:T(8,128)(2,1)} %param.5), channel_id=1, source_target_pairs={{0,4},{1,5},{2,6},{3,7},{4,0},{5,1},{6,2},{7,3},{8,12},{9,13},{10,... | collective-permute-start | bytes 786440 | tf_op jit(solution)/shard_map/ppermute | solution.py:8
  20.1 88.4 %collective-permute-start.3 = (bf16[256,512]{1,0:T(8,128)(2,1)}, bf16[256,512]{1,0:T(8,128)(2,1)S(1)}, u32[]{:S(2)}, u32[]{:S(2)}) collective-permute-start(bf16[256,512]{1,0:T(8,128)(2,1)} %param.5), channel_id=1, source_target_pairs={{0,8},{1,9},{2,10},{3,11},{4,12},{5,13},{6,14},{7,15},{8,0},{9,1},... | collective-permute-start | bytes 786440 | tf_op jit(solution)/shard_map/ppermute | solution.py:8
  25.0 200.2 %reduce-scatter.10.cloned.1.call-start = ((), (), s32[]{:S(2)}) async-start(), calls=%async_computation.8 | async-start | bytes 2359296
  26.2 82.5 %copy-start.7 = (bf16[256,4,2,1,64]{0,4,2,1,3:T(8,128)(2,1)}, bf16[256,4,2,1,64]{0,4,2,1,3:T(8,128)(2,1)S(1)}, u32[]{:S(2)}) copy-start(bf16[256,4,2,1,64]{0,4,2,1,3:T(8,128)(2,1)S(1)} %rev.24) | copy-start | bytes 786436
  26.2 84.0 %copy-start.5 = (bf16[256,2,2,2,64]{0,4,3,2,1:T(8,128)(2,1)}, bf16[256,2,2,2,64]{0,4,3,2,1:T(8,128)(2,1)S(1)}, u32[]{:S(2)}) copy-start(bf16[256,2,2,2,64]{0,4,3,2,1:T(8,128)(2,1)S(1)} %rev.25) | copy-start | bytes 786436
  108.3 4.0 copy-start.11
  108.5 4.3 %copy-start.13 = (bf16[256,512]{0,1:T(8,128)(2,1)}, bf16[256,512]{0,1:T(8,128)(2,1)S(1)}, u32[]{:S(2)}) copy-start(bf16[256,512]{0,1:T(8,128)(2,1)S(1)} %copy.83) | copy-start | bytes 786436
  116.0 5.5 %copy-start.8 = (bf16[256,4,2,1,64]{0,4,2,1,3:T(8,128)(2,1)S(1)}, bf16[256,4,2,1,64]{0,4,2,1,3:T(8,128)(2,1)}, u32[]{:S(2)}) copy-start(bf16[256,4,2,1,64]{0,4,2,1,3:T(8,128)(2,1)} %copy-done.7) | copy-start | bytes 786436
  125.4 126.0 %reduce-scatter.6.cloned.1.call-start = ((), (), s32[]{:S(2)}) async-start(), calls=%async_computation.6 | async-start | bytes 294912 | tf_op jit(solution)/shard_map/reduce_scatter | solution.py:85
  190.9 101.8 %reduce-scatter.8.cloned.1.call-start = ((), (), s32[]{:S(2)}) async-start(), calls=%async_computation.7 | async-start | bytes 1179648 | tf_op jit(solution)/shard_map/reduce_scatter | solution.py:86
  192.4 199.5 %all-reduce.6.cloned.1.call-start = ((), (), s32[]{:S(2)}) async-start(), calls=%async_computation.5 | async-start | bytes 1048576 | tf_op jit(solution)/shard_map/psum | solution.py:88
  206.6 17.8 %collective-permute-start.4 = (bf16[256,8,64]{0,2,1:T(8,128)(2,1)}, bf16[256,8,64]{0,2,1:T(8,128)(2,1)S(1)}, u32[]{:S(2)}, u32[]{:S(2)}) collective-permute-start(bf16[256,8,64]{0,2,1:T(8,128)(2,1)} %fusion.14), channel_id=1, source_target_pairs={{0,1},{1,0},{2,3},{3,2},{4,5},{5,4},{6,7},{7,6},{8,9},{9,8},{10,11... | collective-permute-start | bytes 786440 | tf_op jit(solution)/shard_map/ppermute | solution.py:8
  209.9 13.5 %copy-start.2 = (f32[256,512]{1,0:T(8,128)S(1)}, f32[256,512]{1,0:T(8,128)}, u32[]{:S(2)}) copy-start(f32[256,512]{1,0:T(8,128)} %copy.93) | copy-start | bytes 1572868
  209.9 13.4 %copy-start.3 = (f32[256,512]{1,0:T(8,128)S(1)}, f32[256,512]{1,0:T(8,128)}, u32[]{:S(2)}) copy-start(f32[256,512]{1,0:T(8,128)} %copy.87) | copy-start | bytes 1572868
  209.9 14.6 %collective-permute-start.5 = (bf16[256,8,64]{0,2,1:T(8,128)(2,1)S(1)}, bf16[256,8,64]{0,2,1:T(8,128)(2,1)S(1)}, u32[]{:S(2)}, u32[]{:S(2)}) collective-permute-start(bf16[256,8,64]{0,2,1:T(8,128)(2,1)S(1)} %fusion.15), channel_id=1, source_target_pairs={{0,2},{1,3},{2,0},{3,1},{4,6},{5,7},{6,4},{7,5},{8,10},{9,11},{10,... | collective-permute-start | bytes 786440 | tf_op jit(solution)/shard_map/ppermute | solution.py:8
  213.3 11.2 %collective-permute-start.6 = (bf16[256,8,64]{0,2,1:T(8,128)(2,1)S(1)}, bf16[256,8,64]{0,2,1:T(8,128)(2,1)S(1)}, u32[]{:S(2)}, u32[]{:S(2)}) collective-permute-start(bf16[256,8,64]{0,2,1:T(8,128)(2,1)S(1)} %fusion.16), channel_id=1, source_target_pairs={{0,4},{1,5},{2,6},{3,7},{4,0},{5,1},{6,2},{7,3},{8,12},{9,13},{10,... | collective-permute-start | bytes 786440 | tf_op jit(solution)/shard_map/ppermute | solution.py:8
  217.4 12.4 %collective-permute-start.7 = (bf16[256,8,64]{0,2,1:T(8,128)(2,1)}, bf16[256,8,64]{0,2,1:T(8,128)(2,1)S(1)}, u32[]{:S(2)}, u32[]{:S(2)}) collective-permute-start(bf16[256,8,64]{0,2,1:T(8,128)(2,1)} %fusion.17), channel_id=1, source_target_pairs={{0,8},{1,9},{2,10},{3,11},{4,12},{5,13},{6,14},{7,15},{8,0},{9,1},... | collective-permute-start | bytes 786440 | tf_op jit(solution)/shard_map/ppermute | solution.py:8
  225.2 4.9 %copy-start.4 = (f32[256,512]{1,0:T(8,128)S(1)}, f32[256,512]{1,0:T(8,128)}, u32[]{:S(2)}) copy-start(f32[256,512]{1,0:T(8,128)} %fusion.12) | copy-start | bytes 1572868
  (7 other events, 10.7 us)
Sparse Core Ops, SparseCore 0:
  10.1 41.0 all-gather.2
  53.4 31.9 all-gather.4
  125.6 49.0 reduce-scatter.9
  191.0 60.4 reduce-scatter.5
  254.4 38.2 reduce-scatter.7
  295.7 96.2 all-reduce.5
where the time goes:
time: 402 us; the launch traced here: 401 us
  blocking collectives  187 us (47%)
  waiting for transfers between devices  121 us (30%)
  matrix products  31.2 us (8%)
  starting transfers between devices  29.2 us (7%)
  local copies, waits for them, and re-layouts  14.9 us (4%)
  between operations  14.7 us (4%)
    psum x1, blocking collectives, local(): lowrank = lax.psum(low_part, 'tensor').astype(jnp.bfloat16)  66.5 us
    psum x1, blocking collectives, local(): glow = lax.psum(glow_part, 'tensor').astype(jnp.bfloat16)  62.8 us
    psum x1, waiting for transfers between devices, local(): lax.psum((shard_bfly, shard_left, shard_right), 'dp')  56.5 us
    psum x1, blocking collectives, local(): lax.psum((shard_bfly, shard_left, shard_right), 'dp')  42.8 us
    reduce_scatter x1, waiting for transfers between devices, local(): lax.psum_scatter(part_right, 'fsdp', scatter_dimension=0, tiled=True)  41.2 us
    ppermute x8, starting transfers between devices, swapped(): lax.ppermute(shard, axis, [(i, i ^ 1 << distance) for i in range(lax.axis...  28.8 us
    reduce_scatter x1, waiting for transfers between devices, local(): lax.psum_scatter(part_left, 'fsdp', scatter_dimension=1, tiled=True)  20.4 us
    all_gather x1, blocking collectives, local(): lax.all_gather(left_factor, 'fsdp', axis=1, tiled=True)  14.9 us
  transfers between devices with their start and end apart: 14, of which 4 were waited for; matrix products, arithmetic and copies ran while one was open for 9% of the time, Pallas kernels for 0%

commit v1 on v0

v1 whole, which is shorter than its diff:
```python
import jax
import jax.numpy as jnp
from jax import lax
from jax.experimental import pallas as pl
from jax.experimental.pallas import tpu as pltpu
from jax.sharding import PartitionSpec as P

F32, BF16 = jnp.float32, jnp.bfloat16
TOK, PAIRS, LANES = 256, 4, 128
KZ, NH = 1152, 512
ROWS, COLS = 192, 256
LROWS, LCOLS = 32, 512
GELU_A, GELU_B = 0.7978845608028654, 0.044715
NT = (((1,), (1,)), ((), ()))


def rdma(src, dst, send_sem, recv_sem, device):
    return pltpu.make_async_remote_copy(
        src_ref=src,
        dst_ref=dst,
        send_sem=send_sem,
        recv_sem=recv_sem,
        device_id=device,
        device_id_type=pl.DeviceIdType.MESH,
    )


def flip(v, bits):
    if bits == 1:
        return v + 1 - 2 * lax.rem(v, 2)
    if bits == 2:
        return lax.rem(v + 2, 4)
    return 3 - v


class Place:
    def __init__(self):
        dp, fsdp, tensor = lax.axis_index("dp"), lax.axis_index("fsdp"), lax.axis_index("tensor")
        self.z, self.x, self.k = dp, lax.div(fsdp, 2), lax.rem(fsdp, 2)
        zl, y = lax.div(tensor, 4), lax.rem(tensor, 4)
        self.y = y
        self.xright, self.xleft, self.xfar = (lax.rem(self.x + i, 4) for i in (1, 3, 2))
        self.zright, self.zleft, self.zfar = (lax.rem(self.z + i, 4) for i in (1, 3, 2))
        self.sib = (dp, 2 * self.x + 1 - self.k, tensor)
        self.xr = (dp, 2 * self.xright + self.k, tensor)
        self.xl = (dp, 2 * self.xleft + self.k, tensor)
        self.zr = (self.zright, fsdp, tensor)
        self.zl = (self.zleft, fsdp, tensor)
        self.ys = [(dp, fsdp, zl * 4 + flip(y, j)) for j in (1, 2, 3)]
        self.zs = [(dp, fsdp, flip(zl, j) * 4 + y) for j in (1, 2, 3)]
        self.levels = [self.ys[0], self.ys[1], self.zs[0], self.zs[1]]
        self.all = [self.sib, self.xr, self.xl, self.zr, self.zl] + self.ys + self.zs


class Gather:
    def __init__(self, me, src, buf, ss, rs, rows):
        self.me, self.src, self.buf, self.ss, self.rs, self.half = me, src, buf, ss, rs, rows // 2

    def copy(self, i, device):
        me, buf, h = self.me, self.buf, self.half
        src = self.src if i in (0, 1, 4) else None
        ref = {
            0: lambda: buf.at[me.x, me.k],
            1: lambda: buf.at[me.x, me.k],
            2: lambda: buf.at[me.xleft, me.k, pl.ds(0, h)],
            3: lambda: buf.at[me.xright, me.k, pl.ds(h, h)],
            4: lambda: buf.at[me.x, me.k],
            5: lambda: buf.at[me.xleft, me.k],
            6: lambda: buf.at[me.xright, me.k],
            7: lambda: buf.at[me.xfar, me.k],
        }[i]()
        return rdma(ref if src is None else src, ref, self.ss.at[i], self.rs.at[i], device)

    def first(self):
        me = self.me
        self.copy(0, me.xr).start()
        self.copy(1, me.xl).start()
        self.copy(4, me.sib).start()

    def second(self):
        me = self.me
        self.wait(0)
        self.copy(2, me.xr).start()
        self.copy(5, me.sib).start()
        self.wait(1)
        self.copy(3, me.xl).start()
        self.copy(6, me.sib).start()

    def third(self):
        self.wait(2)
        self.wait(3)
        self.copy(7, self.me.sib).start()

    def last(self):
        for i in (4, 5, 6, 7):
            self.wait(i)

    def wait(self, i):
        self.copy(i, self.me.sib).wait_recv()

    def wait_sends(self):
        for i in range(8):
            self.copy(i, self.me.sib).wait_send()


def add(*parts):
    total = parts[0].astype(F32)
    for part in parts[1:]:
        total = total + part.astype(F32)
    return total


class Reduce:
    def __init__(self, me, bufs, ss, rs, half, split):
        self.me, self.ss, self.rs, self.half, self.split = me, ss, rs, half, split
        self.part, self.fromsib, self.sums, self.h1, self.h2, self.b, self.z1, self.z2, self.g = bufs

    def ends(self, i):
        me, h = self.me, self.half
        return {
            0: lambda: (self.part.at[1 - me.k], self.fromsib, me.sib),
            1: lambda: (self.sums.at[me.xfar, pl.ds(0, h)], self.h1.at[0], me.xr),
            2: lambda: (self.sums.at[me.xfar, pl.ds(h, h)], self.h1.at[1], me.xl),
            3: lambda: (self.sums.at[me.xright], self.h2.at[0], me.xr),
            4: lambda: (self.sums.at[me.xleft], self.h2.at[1], me.xl),
            5: lambda: (self.b.at[me.zfar, 0], self.z1.at[0], me.zr),
            6: lambda: (self.b.at[me.zfar, 1], self.z1.at[1], me.zl),
            7: lambda: (self.b.at[me.zright], self.z2.at[0], me.zr),
            8: lambda: (self.b.at[me.zleft], self.z2.at[1], me.zl),
            9: lambda: (self.g.at[me.z], self.g.at[me.z], me.zr),
            10: lambda: (self.g.at[me.z], self.g.at[me.z], me.zl),
            11: lambda: (self.g.at[me.zleft, 0], self.g.at[me.zleft, 0], me.zr),
            12: lambda: (self.g.at[me.zright, 1], self.g.at[me.zright, 1], me.zl),
        }[i]()

    def send(self, i):
        src, dst, device = self.ends(i)
        rdma(src, dst, self.ss.at[i], self.rs.at[i], device).start()

    def wait(self, i):
        src, dst, device = self.ends(i)
        rdma(src, dst, self.ss.at[i], self.rs.at[i], device).wait_recv()

    def wait_sends(self):
        for i in range(13):
            src, dst, device = self.ends(i)
            rdma(src, dst, self.ss.at[i], self.rs.at[i], device).wait_send()

    def s1(self):
        self.wait(0)
        for i in range(4):
            self.sums[i] = add(self.part[self.me.k, i], self.fromsib[i]).astype(BF16)
        self.send(1)
        self.send(2)

    def s2(self):
        me, h = self.me, self.half
        self.wait(1)
        self.sums[me.xright, 0:h] = add(self.sums[me.xright, 0:h], self.h1[0]).astype(BF16)
        self.send(3)
        self.wait(2)
        self.sums[me.xleft, h : 2 * h] = add(self.sums[me.xleft, h : 2 * h], self.h1[1]).astype(BF16)
        self.send(4)

    def s3(self):
        me = self.me
        self.wait(3)
        self.wait(4)
        total = add(self.sums[me.x], self.h2[0], self.h2[1])
        for q in range(4):
            for h in range(2):
                self.b[q, h] = self.split(total, q, h).astype(BF16)
        self.send(5)
        self.send(6)

    def s4(self):
        me = self.me
        self.wait(5)
        self.b[me.zright, 0] = add(self.b[me.zright, 0], self.z1[0]).astype(BF16)
        self.send(7)
        self.wait(6)
        self.b[me.zleft, 1] = add(self.b[me.zleft, 1], self.z1[1]).astype(BF16)
        self.send(8)

    def s5(self):
        me = self.me
        self.wait(7)
        self.wait(8)
        self.g[me.z] = add(self.b[me.z], self.z2[0], self.z2[1]).astype(BF16)
        self.send(9)
        self.send(10)

    def s6(self):
        self.wait(9)
        self.send(11)
        self.wait(10)
        self.send(12)

    def s7(self):
        self.wait(11)
        self.wait(12)


class Sum:
    def __init__(self, me, part, s1, r1, s2, r2, out, ss, rs):
        self.me, self.part, self.s1, self.r1, self.s2, self.r2, self.out = me, part, s1, r1, s2, r2, out
        self.ss, self.rs = ss, rs

    def copy(self, step, j):
        me = self.me
        src, dst, device = {
            0: lambda: (self.s1.at[flip(me.y, j + 1)], self.r1.at[j], me.ys[j]),
            1: lambda: (self.s2, self.r2.at[j], me.zs[j]),
            2: lambda: (self.out.at[me.y], self.out.at[me.y], me.ys[j]),
        }[step]()
        return rdma(src, dst, self.ss.at[step * 3 + j], self.rs.at[step * 3 + j], device)

    def t1(self):
        for q in range(4):
            self.s1[q] = self.part[q].astype(BF16)
        for j in range(3):
            self.copy(0, j).start()

    def t2(self):
        for j in range(3):
            self.copy(0, j).wait_recv()
        total = add(self.part[self.me.y], *[self.r1[j] for j in range(3)])
        self.part[self.me.y] = total
        self.s2[...] = total.astype(BF16)
        for j in range(3):
            self.copy(1, j).start()

    def t3(self):
        for j in range(3):
            self.copy(1, j).wait_recv()
        self.out[self.me.y] = add(self.part[self.me.y], *[self.r2[j] for j in range(3)]).astype(BF16)
        for j in range(3):
            self.copy(2, j).start()

    def t4(self):
        for j in range(3):
            self.copy(2, j).wait_recv()

    def wait_sends(self):
        for step in range(3):
            for j in range(3):
                self.copy(step, j).wait_send()


def kernel(
    feat_ref, cot_ref, w_ref, left_ref, act_ref, fg_ref, bg_ref, lgr_ref, rg_ref,
    xall, wg, lgat, wz, xt, lowt, part, t_s1, t_r1, t_s2, t_r2, lowq, pre, gp, dfeat, ds_, dr_,
    m_p, m_sr, m_a, m_h1, m_h2, m_b, m_z1, m_z2, m_g,
    l_p, l_sr, l_a, l_h1, l_h2, l_b, l_z1, l_z2, l_g,
    ga_s, ga_r, rd_s, rd_r, su_s, su_r, x_s, x_r, d_s, d_r,
):
    me = Place()
    barrier = pltpu.get_barrier_semaphore()
    for device in me.all:
        pl.semaphore_signal(barrier, inc=1, device_id=device, device_id_type=pl.DeviceIdType.MESH)

    for p in range(PAIRS):
        xall[0, p] = feat_ref[:, p * LANES : (p + 1) * LANES]
    lgat[me.x, me.k] = left_ref[...]
    for c in range(PAIRS):
        wg[c, me.x, me.k] = w_ref[c]
    pl.semaphore_wait(barrier, len(me.all))

    gather_left = Gather(me, left_ref, lgat, ga_s.at[4], ga_r.at[4], LROWS)

    def gather(c):
        return Gather(me, w_ref.at[c], wg.at[c], ga_s.at[c], ga_r.at[c], ROWS)

    def level(j):
        return rdma(xall.at[0], xall.at[j + 1], x_s.at[j], x_r.at[j], me.levels[j])

    def term(j, c):
        return rdma(ds_.at[j, c], dr_.at[j, c], d_s.at[j, c], d_r.at[j, c], me.levels[j])

    def total(a):
        return Sum(
            me, part.at[a], t_s1.at[a], t_r1.at[a], t_s2.at[a], t_r2.at[a], lowq.at[a], su_s.at[a], su_r.at[a]
        )

    def split_main(v, q, h):
        return v[48 * q : 48 * q + 48, LANES * h : LANES * (h + 1)]

    def split_left(v, q, h):
        return v[16 * h : 16 * h + 16, LANES * q : LANES * (q + 1)]

    def reduce_main(c):
        bufs = [r.at[c] for r in (m_p, m_sr, m_a, m_h1, m_h2, m_b, m_z1, m_z2, m_g)]
        return Reduce(me, bufs, rd_s.at[c], rd_r.at[c], ROWS // 2, split_main)

    reduce_left = Reduce(
        me, (l_p, l_sr, l_a, l_h1, l_h2, l_b, l_z1, l_z2, l_g), rd_s.at[4], rd_r.at[4], LROWS // 2, split_left
    )

    gather_left.first()
    for j in range(4):
        level(j).start()
    for c in range(PAIRS):
        gather(c).first()

    def clear(i, carry):
        wz[lax.div(i, 9), pl.ds(lax.rem(i, 9) * 128, 128), :] = jnp.zeros((128, NH), BF16)
        return carry

    lax.fori_loop(0, PAIRS * 9, clear, 0)
    dfeat[...] = jnp.zeros_like(dfeat)
    part[1] = jnp.zeros((4, 64, 256), F32)

    gather_left.second()
    gather_left.third()
    gather_left.last()
    features = jnp.concatenate([xall[0, p] for p in range(PAIRS)], axis=1)
    low_part = lax.dot_general(features, lgat[...].reshape(256, 512), NT, preferred_element_type=F32)
    part[0] = low_part.reshape(4, 64, 256)
    total(0).t1()
    gather(0).second()
    gather(1).second()
    total(0).t2()
    gather(2).second()
    gather(3).second()
    gather(0).third()
    total(0).t3()
    for c in range(1, PAIRS):
        gather(c).third()
    for j in range(4):
        level(j).wait_recv()

    def turn(c, carry):
        for j in range(7):
            if j == 0:
                tile = xall[0, c]
            elif j == 1:
                tile = xall[0, flip(c, 1)]
            elif j == 2:
                tile = xall[0, flip(c, 2)]
            else:
                tile = xall[j - 2, c]
            turned = tile.T
            if j == 0:
                for gi in range(2):
                    xt[2 * c + gi, 0:64, :] = turned[64 * gi : 64 * gi + 64]
                    xt[2 * c + gi, 64:128, :] = turned[64 * (1 - gi) : 64 * (1 - gi) + 64]
            else:
                for gi in range(2):
                    xt[2 * c + gi, 64 * (j + 1) : 64 * (j + 2), :] = turned[64 * gi : 64 * gi + 64]
        return carry

    lax.fori_loop(0, PAIRS, turn, 0)
    total(0).t4()
    lowt[...] = lowq[0].reshape(256, 256).T

    def compute(c):
        gather(c).last()
        for gi in range(2):
            block = wg[c, :, :, 64 * gi : 64 * gi + 64, :].astype(F32).reshape(8, 64, COLS)
            for t in range(8):
                row = gi * 64 if t == 0 else (1 - gi) * 64 if t == 1 else (t - 1) * LANES + gi * 64
                rows = block[:, 8 * t : 8 * t + 8, :].reshape(64, COLS).astype(BF16)
                wz[c, row : row + 64, COLS * gi : COLS * (gi + 1)] = rows
            right = wg[c, :, :, 128 + 32 * gi : 160 + 32 * gi, :].reshape(256, COLS)
            wz[c, 896:1152, COLS * gi : COLS * (gi + 1)] = right
        tiles = [xall[0, c], xall[0, flip(c, 1)], xall[0, flip(c, 2)]] + [xall[j, c] for j in range(1, 5)]
        xcat = jnp.concatenate(tiles + [lowq[0].reshape(256, 256)], axis=1)
        pre[...] = jnp.dot(xcat, wz[c], preferred_element_type=F32)

        def gelu(i, carry):
            rows = pl.ds(i * 32, 32)
            cols = pl.ds(pl.multiple_of(c * NH, NH), NH)
            v = pre[rows, :]
            th = jnp.tanh(GELU_A * (v + GELU_B * (v * v * v)))
            half = 0.5 * (1.0 + th)
            act_ref[rows, cols] = (v * half).astype(BF16)
            slope = half + 0.5 * v * (1.0 - th * th) * (GELU_A * (1.0 + 3.0 * GELU_B * (v * v)))
            gp[rows, :] = (cot_ref[rows, cols].astype(F32) * slope).astype(BF16)
            return carry

        lax.fori_loop(0, 8, gelu, 0)

        for gi in range(2):
            g = gp[:, COLS * gi : COLS * (gi + 1)]
            grad = jnp.dot(xt[2 * c + gi], g, preferred_element_type=F32).reshape(4, 2, 8, 8, COLS)
            for tp in range(4):
                for f in range(8):
                    rows = jnp.concatenate([grad[tp, 0, f], grad[tp, 1, f]], axis=0).astype(BF16)
                    m_p[c, f % 2, f // 2, 64 * gi + 16 * tp : 64 * gi + 16 * tp + 16, :] = rows
            grad = jnp.dot(lowt[...], g, preferred_element_type=F32).astype(BF16)
            for f in range(8):
                m_p[c, f % 2, f // 2, 128 + 32 * gi : 160 + 32 * gi, :] = grad[32 * f : 32 * f + 32]
        reduce_main(c).send(0)

        def back(first, last):
            return lax.dot_general(gp[...], wz[c, first:last, :], NT, preferred_element_type=F32)

        far = back(384, 640)
        for j in range(2):
            ds_[j, c] = far[:, LANES * j : LANES * (j + 1)].astype(BF16)
            term(j, c).start()
        far = back(640, 896)
        for j in range(2):
            ds_[j + 2, c] = far[:, LANES * j : LANES * (j + 1)].astype(BF16)
            term(j + 2, c).start()
        near = back(0, 256)
        dfeat[c] += near[:, :LANES]
        dfeat[flip(c, 1)] += near[:, LANES:]
        dfeat[flip(c, 2)] += back(256, 384)
        part[1] += back(896, 1152).reshape(4, 64, 256)

    def write_main(c):
        for_q = [jnp.concatenate([m_g[c, q, 0].astype(F32), m_g[c, q, 1].astype(F32)], axis=1) for q in range(4)]
        rows = jnp.concatenate(for_q, axis=0)
        for gi in range(2):
            for t in range(8):
                first = 64 * gi + 8 * t
                bg_ref[t, 2 * c + gi] = rows[first : first + 8]
            cols = pl.ds(pl.multiple_of((2 * c + gi) * COLS, COLS), COLS)
            rg_ref[:, cols] = rows[128 + 32 * gi : 160 + 32 * gi]

    def left_start():
        glow = lowq[1].reshape(256, 256)
        mine = jnp.concatenate([xall[0, p] for p in range(PAIRS)], axis=1)
        grad = jnp.dot(glow.T, mine, preferred_element_type=F32).astype(BF16)
        for f in range(8):
            l_p[f % 2, f // 2] = grad[LROWS * f : LROWS * (f + 1)]
        reduce_left.send(0)

    def feature_grad():
        for j in range(4):
            for c in range(PAIRS):
                term(j, c).wait_recv()
        glow = lowq[1].reshape(256, 256)
        low = jnp.dot(glow, lgat[...].reshape(256, 512), preferred_element_type=F32)
        for c in range(PAIRS):
            cols = slice(LANES * c, LANES * (c + 1))
            fg_ref[:, cols] = add(low[:, cols], dfeat[c], *[dr_[j, c] for j in range(4)]).astype(BF16)

    def write_left():
        for q in range(4):
            for h in range(2):
                lgr_ref[16 * h : 16 * h + 16, LANES * q : LANES * (q + 1)] = l_g[q, h].astype(F32)

    left_at = 6

    def tick(i, carry):
        for step in range(7, 0, -1):

            @pl.when(i == left_at + step)
            def _(step=step):
                getattr(reduce_left, f"s{step}")()
                if step == 7:
                    write_left()

        @pl.when(i == 4)
        def _():
            total(1).t2()

        @pl.when(i == 5)
        def _():
            total(1).t3()

        @pl.when(i == 6)
        def _():
            total(1).t4()
            left_start()

        for step in range(7, 0, -1):
            c = i - step

            @pl.when((c >= 0) & (c < PAIRS))
            def _(step=step, c=c):
                getattr(reduce_main(c), f"s{step}")()
                if step == 7:
                    write_main(c)

        @pl.when(i < PAIRS)
        def _():
            compute(i)

        @pl.when(i == PAIRS - 1)
        def _():
            total(1).t1()

        @pl.when(i == 9)
        def _():
            feature_grad()

        return carry

    lax.fori_loop(0, left_at + 8, tick, 0)

    gather_left.wait_sends()
    reduce_left.wait_sends()
    for a in range(2):
        total(a).wait_sends()
    for j in range(4):
        level(j).wait_send()

    def drain(c, carry):
        gather(c).wait_sends()
        reduce_main(c).wait_sends()
        for j in range(4):
            term(j, c).wait_send()
        return carry

    lax.fori_loop(0, PAIRS, drain, 0)


def local(features, cotangent, butterfly, left_factor, right_factor):
    rows = butterfly.transpose(1, 0, 2, 3).reshape(PAIRS, 128, COLS)
    right = right_factor.reshape(32, 8, COLS).transpose(1, 0, 2).reshape(PAIRS, 64, COLS)
    shard = jnp.concatenate([rows, right], axis=1)
    vmem = pltpu.VMEM
    dma = pltpu.SemaphoreType.DMA
    scratch = [
        vmem((5, 4, TOK, LANES), BF16),
        vmem((4, 4, 2, ROWS, COLS), BF16),
        vmem((4, 2, LROWS, LCOLS), BF16),
        vmem((4, KZ, NH), BF16),
        vmem((8, 512, TOK), BF16),
        vmem((256, 256), BF16),
        vmem((2, 4, 64, 256), F32),
        vmem((2, 4, 64, 256), BF16),
        vmem((2, 3, 64, 256), BF16),
        vmem((2, 64, 256), BF16),
        vmem((2, 3, 64, 256), BF16),
        vmem((2, 4, 64, 256), BF16),
        vmem((TOK, NH), F32),
        vmem((TOK, NH), BF16),
        vmem((4, TOK, LANES), F32),
        vmem((4, 4, TOK, LANES), BF16),
        vmem((4, 4, TOK, LANES), BF16),
    ]
    for lead, r, c, quarter in (((4,), ROWS, COLS, 48), ((), LROWS, LCOLS, 16)):
        scratch += [
            vmem(lead + (2, 4, r, c), BF16),
            vmem(lead + (4, r, c), BF16),
            vmem(lead + (4, r, c), BF16),
            vmem(lead + (2, r // 2, c), BF16),
            vmem(lead + (2, r, c), BF16),
            vmem(lead + (4, 2, quarter, LANES), BF16),
            vmem(lead + (2, quarter, LANES), BF16),
            vmem(lead + (2, 2, quarter, LANES), BF16),
            vmem(lead + (4, 2, quarter, LANES), BF16),
        ]
    for shape in ((5, 8), (5, 13), (2, 9), (4,), (4, 4)):
        scratch += [dma(shape), dma(shape)]
    act, fg, bg, lg, rg = pl.pallas_call(
        kernel,
        out_shape=[
            jax.ShapeDtypeStruct((TOK, 2048), BF16),
            jax.ShapeDtypeStruct((TOK, 512), BF16),
            jax.ShapeDtypeStruct((8, 8, 8, 256), F32),
            jax.ShapeDtypeStruct((LROWS, LCOLS), F32),
            jax.ShapeDtypeStruct((32, 2048), F32),
        ],
        in_specs=[pl.BlockSpec(memory_space=vmem)] * 4,
        out_specs=[pl.BlockSpec(memory_space=vmem)] * 5,
        scratch_shapes=scratch,
        compiler_params=pltpu.CompilerParams(
            collective_id=0, has_side_effects=True, vmem_limit_bytes=48 * 1024 * 1024
        ),
        cost_estimate=pl.CostEstimate(flops=4_000_000_000, bytes_accessed=6_000_000, transcendentals=600_000),
    )(features, cotangent, shard, left_factor.T)
    return act, fg, bg, lg.T, rg


def solution(mesh):
    specs = (
        P(("dp", "fsdp"), "tensor"),
        P(("dp", "fsdp"), "tensor"),
        P(None, "tensor", "fsdp", None),
        P("tensor", "fsdp"),
        P("fsdp", "tensor"),
    )
    return jax.shard_map(local, mesh=mesh, in_specs=specs, out_specs=specs, check_vma=False)
```

time: 402 us -> 119 us (0.30)
  the two profiles are of different devices: /device:TPU:1 before, /device:TPU:32 now
where the time goes in v1:
time: 119 us
  Pallas kernels  112 us (94%)
  local copies, waits for them, and re-layouts  6.67 us (6%)
    pallas_call x1, Pallas kernels, local(): pl.pallas_call(kernel, out_shape=[jax.ShapeDtypeStruct((TOK, 2048), BF16)...  112 us
    unnamed x11, local copies, waits for them, and re-layouts  4.7 us

profile of v1, /device:TPU:32, one launch (start us, length us, event | category | flops | bytes accessed | tf_op | source)
XLA Modules:
  0.0 119.0 jit_solution(14464067840621698763)
XLA Ops:
  0.6 0.0 copy-start
  0.6 1.0 copy.14
  1.6 1.0 copy.10
  2.6 0.0 copy-start.1
  2.6 0.0 copy-start.2
  2.7 0.0 copy-done
  2.7 0.9 copy-done.1
  3.6 0.0 copy-done.2
  3.6 111.7 %shard_map.92 = (bf16[256,2048]{1,0:T(8,128)(2,1)S(1)}, bf16[256,512]{1,0:T(8,128)(2,1)S(1)}, f32[8,8,8,256]{3,2,1,0:T(8,128)S(1)}, f32[32,512]{1,0:T(8,128)S(1)}, f32[32,2048]{1,0:T(8,128)S(1)}) custom-call(bf16[256,512]{1,0:T(8,128)(2,1)S(1)} %copy-done.1, bf16[256,2048]{1,0:T(8,128)(2,1)S(1)} %copy-done, bf16[4,192,256]{2,1,0:T(8,128)(2,1)S(1)} %pad_maximum_fusion.w_ref, ...), custom_call_target="tpu_custom_call" | custom-call | flops 4000000000 | bytes 6000000 | tf_op jit(solution)/shard_map/pallas_call | solution.py:550
  115.2 1.0 copy.20
  116.2 0.7 copy.21
  116.9 0.8 copy.22
  117.7 0.6 copy.23
  118.3 0.7 copy.24
  (1 shorter events, 0.0 us)
Async XLA Ops:
  0.6 2.0 %copy-start = (bf16[256,2048]{1,0:T(8,128)(2,1)S(1)}, bf16[256,2048]{1,0:T(8,128)(2,1)}, u32[]{:S(2)}) copy-start(bf16[256,2048]{1,0:T(8,128)(2,1)} %cot_ref.1) | copy-start | bytes 3145732
  2.6 1.0 copy-start.1
  2.6 0.9 copy-start.2
